TPU v7x, 32 devices: a whole 2x2x4 slice. The times are simulated.
32 devices in a mesh: groups: 2 (over x), tile: 16 (over z, y, core).
Axes of the slice: x: 2, y: 2, z: 4, core: 2. Of those that a mesh axis runs over, the one named last changes fastest.
Arguments:
- log_conductivity: float32 [4, 128, 1024], P('groups', 'tile'), parts along dimension 0, may hold values from -2.9 to 3, as said below
- storage: float32 [4, 128, 1024], P('groups', 'tile'), parts along dimension 0, may hold values from 0.05 to 60
- recharge: float32 [4, 128, 1024], P('groups', 'tile'), parts along dimension 0, may hold values from -6 to 6
- observed: float32 [24, 400], P('groups'), parts along dimension 0, may hold values from -6 to 6
- rates: float32 [24], P('groups'), parts along dimension 0, may hold values from 2 to 8
- well_tile: int32 [400], replicated, may hold values from 0 to 15
- well_row: int32 [400], replicated, may hold values from 0 to 7
- well_col: int32 [400], replicated, may hold values from 0 to 1023
- well_screen: int32 [400, 2], replicated, may hold values from 0 to 2, as said below
- test_well: int32 [12], replicated, may hold values from 0 to 399
Outputs:
- gradient: float32 [4, 128, 1024], P('groups', 'tile'), parts along dimension 0
- predicted: float32 [24, 400], P('groups'), parts along dimension 0
There are 2 independent parts, one for each index of `groups`. A program takes and returns all parts, laid end to end along the dimension named above; an argument that names none is the same for every part. Nothing has to cross between parts.
Inputs may be any that keep to these rules, and one draw needn't show every extreme that they name: `log_conductivity`: log-conductivities rough from cell to cell. Each well's screen holds one or more whole layers, well_screen[w,0] < well_screen[w,1].
All inputs are finite; a program needn't handle non-finite values.
Results may differ from a plain program's by a relative error of at most 0.00014.
Values sent between devices are 32-bit elements; how exact they have to be, the bound alone decides.
A program may use at most 64 MiB of HBM per device.

v0:
```python
import jax
import jax.numpy as jnp
from jax import lax
from jax.sharding import PartitionSpec as P

ITERS = 4


def extended_2(block, sides, width):
    for axis, dim in sides:
        count = lax.axis_size(axis)
        forward = [(i, i + 1) for i in range(count - 1)]
        backward = [(target, source) for source, target in forward]
        low = lax.ppermute(
            lax.slice_in_dim(block, block.shape[dim] - width, None, axis=dim), axis, forward
        )
        high = lax.ppermute(lax.slice_in_dim(block, 0, width, axis=dim), axis, backward)
        block = jnp.concatenate([low, block, high], axis=dim)
    return block


def pad_axis(array, axis, before, after):
    widths = [(0, 0)] * array.ndim
    widths[axis] = (before, after)
    return jnp.pad(array, widths)


def faces_along(extended):
    return 0.5 * (extended[:, 1:, :] + extended[:, :-1, :])


def faces_other(conductivity):
    padded_y = pad_axis(conductivity, 2, 1, 1)
    faces_y = 0.5 * (padded_y[:, :, 1:] + padded_y[:, :, :-1])
    faces_z = 0.5 * (conductivity[1:] + conductivity[:-1])
    return (faces_y, faces_z)


def operate(padded, faces_x, faces_y, faces_z, store):
    field = padded[..., 1:-1, :]
    flux_x = faces_x * (padded[..., 1:, :] - padded[..., :-1, :])
    result = store * field + flux_x[..., :-1, :] - flux_x[..., 1:, :]
    padded_y = pad_axis(field, field.ndim - 1, 1, 1)
    flux_y = faces_y * (padded_y[..., 1:] - padded_y[..., :-1])
    result = result + flux_y[..., :-1] - flux_y[..., 1:]
    flux_z = faces_z * (field[..., 1:, :, :] - field[..., :-1, :, :])
    layer_axis = field.ndim - 3
    return result + pad_axis(flux_z, layer_axis, 1, 0) - pad_axis(flux_z, layer_axis, 0, 1)


def chebyshev(source, apply_op, low, high, valid):
    center = 0.5 * (high + low)
    radius = 0.5 * (high - low)
    spread = center / radius
    ratio = 1.0 / spread
    direction = source / center
    iterate = direction
    residual = source
    for turn in range(ITERS):
        residual = residual - apply_op(direction)
        ratio_next = 1.0 / (2.0 * spread - ratio)
        direction = (ratio_next * ratio * direction + 2.0 * ratio_next / radius * residual) * valid
        iterate = iterate + direction
        ratio = ratio_next
    return iterate


def local(
    log_conductivity,
    storage,
    recharge,
    observed,
    rates,
    well_tile,
    well_row,
    well_col,
    well_screen,
    test_well,
):
    layers_count, strip, columns = log_conductivity.shape
    tests = observed.shape[0]
    tile_index = lax.axis_index("tile")
    conductivity = jnp.exp(log_conductivity)
    depth = 1
    coefficients = extended_2(jnp.stack((conductivity, storage)), (("tile", 2),), depth)
    cond_ext = coefficients[0]
    own_x = faces_along(cond_ext)
    own_y, own_z = faces_other(conductivity)
    face_sum = own_x[:, :-1] + own_x[:, 1:] + own_y[:, :, :-1] + own_y[:, :, 1:]
    face_sum = face_sum + pad_axis(own_z, 0, 1, 0) + pad_axis(own_z, 0, 0, 1)
    local_high = jnp.max(storage + 2.0 * face_sum)
    local_low = jnp.min(storage)
    high = lax.pmax(local_high, "tile")
    low = lax.pmin(local_low, "tile")

    def solve(source):
        faces_x = faces_along(cond_ext)
        faces_y, faces_z = faces_other(conductivity)

        def apply_each(field):
            padded = extended_2(field, (("tile", 2),), 1)
            return operate(padded, faces_x, faces_y, faces_z, storage)

        return chebyshev(source, apply_each, low, high, jnp.float32(1.0))

    layers = jnp.arange(layers_count, dtype=jnp.int32)
    top = well_screen[:, 0]
    bottom = well_screen[:, 1]
    inside = ((layers[None, :] >= top[:, None]) & (layers[None, :] < bottom[:, None])).astype(
        jnp.float32
    )
    screen_weight = inside / (bottom - top).astype(jnp.float32)[:, None]
    owned = (well_tile == tile_index).astype(jnp.float32)
    owned_weight = screen_weight * owned[:, None]
    amounts = -rates[:, None] * owned_weight[test_well]
    test_rows = jnp.arange(tests, dtype=jnp.int32)[:, None]
    layer_rows = layers[None, :]
    pumping = jnp.zeros((tests, layers_count, strip, columns), jnp.float32)
    pumping = pumping.at[
        test_rows, layer_rows, well_row[test_well][:, None], well_col[test_well][:, None]
    ].add(amounts)
    heads = solve(recharge[None] + pumping)
    sampled = heads[:, :, well_row, well_col]
    local_heads = jnp.sum(sampled * owned_weight.T[None], axis=1)
    predicted = lax.psum(local_heads, "tile")
    misfit = predicted - observed
    scale = jnp.sqrt(jnp.mean(misfit * misfit) + 1e-06)
    weight = misfit / scale
    adjoint_source = jnp.zeros((tests, layers_count, strip, columns), jnp.float32)
    adjoint_source = adjoint_source.at[:, :, well_row, well_col].add(
        weight[:, None, :] * owned_weight.T[None]
    )
    adjoint = solve(adjoint_source)
    padded = extended_2(jnp.stack((heads, adjoint)), (("tile", 3),), 1)
    term_x = jnp.sum(
        0.5
        * (padded[1][:, :, 1:] - padded[1][:, :, :-1])
        * (padded[0][:, :, 1:] - padded[0][:, :, :-1]),
        axis=0,
    )
    x_sum = term_x[:, :-1] + term_x[:, 1:]
    padded_a = pad_axis(adjoint, 3, 1, 1)
    padded_h = pad_axis(heads, 3, 1, 1)
    term_y = jnp.sum(
        0.5 * (padded_a[..., 1:] - padded_a[..., :-1]) * (padded_h[..., 1:] - padded_h[..., :-1]),
        axis=0,
    )
    term_z = jnp.sum(
        0.5 * (adjoint[:, 1:] - adjoint[:, :-1]) * (heads[:, 1:] - heads[:, :-1]), axis=0
    )
    cell_sum = x_sum + term_y[:, :, :-1] + term_y[:, :, 1:]
    cell_sum = cell_sum + pad_axis(term_z, 0, 1, 0) + pad_axis(term_z, 0, 0, 1)
    gradient = -conductivity * cell_sum
    return (gradient, predicted)


def solution(mesh):
    return jax.shard_map(
        local,
        mesh=mesh,
        in_specs=(
            P("groups", "tile", None),
            P("groups", "tile", None),
            P("groups", "tile", None),
            P("groups", None),
            P("groups"),
            P(),
            P(),
            P(),
            P(),
            P(),
        ),
        out_specs=(P("groups", "tile", None), P("groups", None)),
        check_vma=False,
    )
```

profile of v0, /device:TPU:5, one launch (start us, length us, event | category | flops | bytes accessed | tf_op | source)
XLA Modules:
  0.0 294.1 jit_solution(15009678495756000687)
XLA Ops:
  2.5 3.7 %collective-permute-start = (f32[2,2,1,1024]{3,2,1,0:T(1,128)S(1)}, f32[2,2,1,1024]{3,2,1,0:T(1,128)S(1)}, u32[]{:S(2)}, u32[]{:S(2)}) collective-permute-start(f32[2,2,1,1024]{3,2,1,0:T(1,128)S(1)} %get-tuple-element.40), channel_id=1, source_target_pairs={{0,1},{1,2},{2,3},{3,4},{4,5},{5,6},{6,7},{7,8},{8,9},{9,10},{10,1... | collective-permute-start | bytes 49160 | tf_op jit(solution)/shard_map/ppermute | solution.py:14
  15.8 2.9 scatter_fusion
  19.5 25.8 %pmax.7 = f32[]{:T(128)} all-reduce(f32[]{:T(128)} %get-tuple-element.5), channel_id=1, replica_groups=mesh['groups'=2,'tile'=16] {'tile'}, use_global_device_ids=true, to_apply=%region_2.3 | all-reduce | flops 1 | bytes 8 | tf_op jit(solution)/shard_map/pmax | solution.py:93
  45.4 32.8 %pmin.7 = f32[]{:T(128)} all-reduce(f32[]{:T(128)} %get-tuple-element.4), channel_id=1, replica_groups=mesh['groups'=2,'tile'=16] {'tile'}, use_global_device_ids=true, to_apply=%region_4.5 | all-reduce | flops 1 | bytes 8 | tf_op jit(solution)/shard_map/pmin | solution.py:94
  86.9 2.7 collective-permute-done.2
  93.7 4.0 %collective-permute-start.4 = (f32[12,2,1,1024]{3,2,1,0:T(1,128)S(1)}, f32[12,2,1,1024]{3,2,1,0:T(1,128)S(1)}, u32[]{:S(2)}, u32[]{:S(2)}) collective-permute-start(f32[12,2,1,1024]{3,2,1,0:T(1,128)S(1)} %get-tuple-element.37), channel_id=1, source_target_pairs={{1,0},{2,1},{3,2},{4,3},{5,4},{6,5},{7,6},{8,7},{9,8},{10,9},{11,1... | collective-permute-start | bytes 294920 | tf_op jit(solution)/shard_map/ppermute | solution.py:17
  97.8 2.7 collective-permute-done.4
  103.7 3.3 %collective-permute-start.6 = (f32[12,2,1,1024]{3,2,1,0:T(1,128)S(1)}, f32[12,2,1,1024]{3,2,1,0:T(1,128)S(1)}, u32[]{:S(2)}, u32[]{:S(2)}) collective-permute-start(f32[12,2,1,1024]{3,2,1,0:T(1,128)S(1)} %get-tuple-element.35), channel_id=1, source_target_pairs={{1,0},{2,1},{3,2},{4,3},{5,4},{6,5},{7,6},{8,7},{9,8},{10,9},{11,1... | collective-permute-start | bytes 294920 | tf_op jit(solution)/shard_map/ppermute | solution.py:17
  107.1 3.5 %collective-permute-done.6 = f32[12,2,1,1024]{3,2,1,0:T(1,128)S(1)} collective-permute-done((f32[12,2,1,1024]{3,2,1,0:T(1,128)S(1)}, f32[12,2,1,1024]{3,2,1,0:T(1,128)S(1)}, u32[]{:S(2)}, u32[]{:S(2)}) %collective-permute-start.6) | collective-permute-done | bytes 98336 | tf_op jit(solution)/shard_map/ppermute | solution.py:17
  113.8 2.6 collective-permute-start.8
  116.4 4.2 %collective-permute-done.8 = f32[12,2,1,1024]{3,2,1,0:T(1,128)S(1)} collective-permute-done((f32[12,2,1,1024]{3,2,1,0:T(1,128)S(1)}, f32[12,2,1,1024]{3,2,1,0:T(1,128)S(1)}, u32[]{:S(2)}, u32[]{:S(2)}) %collective-permute-start.8) | collective-permute-done | bytes 98336 | tf_op jit(solution)/shard_map/ppermute | solution.py:17
  121.7 5.9 %copy.25 = f32[12,2,8,1024]{0,1,3,2:T(2,128)} copy(f32[12,2,8,1024]{3,2,1,0:T(8,128)S(1)} %fusion.31) | data formatting | bytes 1572864 | tf_op jit(solution)/shard_map/add | solution.py:63
  127.6 6.5 %gather_fusion.3 = f32[400,12,2]{1,2,0:T(2,128)S(1)} fusion(f32[12,2,8,1024]{0,1,3,2:T(2,128)} %copy.25, s32[400]{0:T(512)S(1)} %bitcast.31), kind=kCustom, calls=%fused_computation.3 | custom fusion | bytes 80000 | tf_op jit(solution)/shard_map/gather | solution.py:123
  134.9 49.3 %psum.7 = f32[12,400]{1,0:T(8,128)S(1)} all-reduce(f32[12,400]{1,0:T(8,128)S(1)} %copy.27), channel_id=1, replica_groups=mesh['groups'=2,'tile'=16] {'tile'}, use_global_device_ids=true, to_apply=%region_6.7 | all-reduce | flops 4800 | bytes 38400 | tf_op jit(solution)/shard_map/psum | solution.py:125
  186.1 5.9 %broadcast.196 = f32[12,2,8,1024]{0,1,3,2:T(2,128)} broadcast(f32[]{:T(128)} %constant.19.clone.1), dimensions={} | broadcast | bytes 786436 | tf_op jit(solution)/shard_map/broadcast.24
  192.1 39.4 %scatter_fusion.1 = f32[12,2,8,1024]{0,1,3,2:T(2,128)} fusion(f32[12,2,8,1024]{0,1,3,2:T(2,128)} %broadcast.196, s32[400]{0:T(512)S(1)} %bitcast.32, f32[400,12,2]{1,2,0:T(2,128)S(1)} %multiply_bitcast_fusion), kind=kCustom, calls=%fused_computation.5 | custom fusion | flops 9600 | bytes 118400 | tf_op jit(solution)/shard_map/scatter-add | solution.py:130
  231.5 6.9 %copy.29 = f32[12,2,8,1024]{3,2,1,0:T(8,128)S(1)} copy(f32[12,2,8,1024]{0,1,3,2:T(2,128)} %scatter_fusion.1) | data formatting | bytes 1572864 | tf_op jit(solution)/shard_map/scatter-add | solution.py:130
  238.9 4.5 %collective-permute-start.11 = (f32[12,2,1,1024]{3,2,1,0:T(1,128)S(1)}, f32[12,2,1,1024]{3,2,1,0:T(1,128)S(1)}, u32[]{:S(2)}, u32[]{:S(2)}) collective-permute-start(f32[12,2,1,1024]{3,2,1,0:T(1,128)S(1)} %get-tuple-element.30), channel_id=1, source_target_pairs={{0,1},{1,2},{2,3},{3,4},{4,5},{5,6},{6,7},{7,8},{8,9},{9,10},{10,1... | collective-permute-start | bytes 294920 | tf_op jit(solution)/shard_map/ppermute | solution.py:14
  243.4 4.3 %collective-permute-start.10 = (f32[12,2,1,1024]{3,2,1,0:T(1,128)S(1)}, f32[12,2,1,1024]{3,2,1,0:T(1,128)S(1)}, u32[]{:S(2)}, u32[]{:S(2)}) collective-permute-start(f32[12,2,1,1024]{3,2,1,0:T(1,128)S(1)} %get-tuple-element.31), channel_id=1, source_target_pairs={{1,0},{2,1},{3,2},{4,3},{5,4},{6,5},{7,6},{8,7},{9,8},{10,9},{11,1... | collective-permute-start | bytes 294920 | tf_op jit(solution)/shard_map/ppermute | solution.py:17
  253.4 3.6 %collective-permute-start.12 = (f32[12,2,1,1024]{3,2,1,0:T(1,128)S(1)}, f32[12,2,1,1024]{3,2,1,0:T(1,128)S(1)}, u32[]{:S(2)}, u32[]{:S(2)}) collective-permute-start(f32[12,2,1,1024]{3,2,1,0:T(1,128)S(1)} %get-tuple-element.29), channel_id=1, source_target_pairs={{1,0},{2,1},{3,2},{4,3},{5,4},{6,5},{7,6},{8,7},{9,8},{10,9},{11,1... | collective-permute-start | bytes 294920 | tf_op jit(solution)/shard_map/ppermute | solution.py:17
  257.1 3.2 %collective-permute-done.12 = f32[12,2,1,1024]{3,2,1,0:T(1,128)S(1)} collective-permute-done((f32[12,2,1,1024]{3,2,1,0:T(1,128)S(1)}, f32[12,2,1,1024]{3,2,1,0:T(1,128)S(1)}, u32[]{:S(2)}, u32[]{:S(2)}) %collective-permute-start.12) | collective-permute-done | bytes 98336 | tf_op jit(solution)/shard_map/ppermute | solution.py:17
  266.1 4.3 %collective-permute-done.14 = f32[12,2,1,1024]{3,2,1,0:T(1,128)S(1)} collective-permute-done((f32[12,2,1,1024]{3,2,1,0:T(1,128)S(1)}, f32[12,2,1,1024]{3,2,1,0:T(1,128)S(1)}, u32[]{:S(2)}, u32[]{:S(2)}) %collective-permute-start.14) | collective-permute-done | bytes 98336 | tf_op jit(solution)/shard_map/ppermute | solution.py:17
  276.1 4.4 %collective-permute-done.16 = f32[12,2,1,1024]{3,2,1,0:T(1,128)S(1)} collective-permute-done((f32[12,2,1,1024]{3,2,1,0:T(1,128)S(1)}, f32[12,2,1,1024]{3,2,1,0:T(1,128)S(1)}, u32[]{:S(2)}, u32[]{:S(2)}) %collective-permute-start.16) | collective-permute-done | bytes 98336 | tf_op jit(solution)/shard_map/ppermute | solution.py:17
  286.8 4.8 %collective-permute-done.19 = f32[2,12,2,1,1024]{4,3,2,1,0:T(1,128)S(1)} collective-permute-done((f32[2,12,2,1,1024]{4,3,2,1,0:T(1,128)S(1)}, f32[2,12,2,1,1024]{4,3,2,1,0:T(1,128)S(1)}, u32[]{:S(2)}, u32[]{:S(2)}) %collective-permute-start.19) | collective-permute-done | bytes 196640 | tf_op jit(solution)/shard_map/ppermute | solution.py:17
  (122 shorter events, 57.8 us)
Async XLA Ops:
  0.6 13.9 %copy-start.5 = (f32[12]{0:T(128)S(1)}, f32[12]{0:T(128)}, u32[]{:S(2)}) copy-start(f32[12]{0:T(128)} %param.14) | copy-start | bytes 148
  0.6 15.1 %copy-start.3 = (f32[2,8,1024]{2,1,0:T(8,128)S(1)}, f32[2,8,1024]{2,1,0:T(8,128)}, u32[]{:S(2)}) copy-start(f32[2,8,1024]{2,1,0:T(8,128)} %param.12) | copy-start | bytes 196612
  2.5 16.2 %collective-permute-start = (f32[2,2,1,1024]{3,2,1,0:T(1,128)S(1)}, f32[2,2,1,1024]{3,2,1,0:T(1,128)S(1)}, u32[]{:S(2)}, u32[]{:S(2)}) collective-permute-start(f32[2,2,1,1024]{3,2,1,0:T(1,128)S(1)} %get-tuple-element.40), channel_id=1, source_target_pairs={{0,1},{1,2},{2,3},{3,4},{4,5},{5,6},{6,7},{7,8},{8,9},{9,10},{10,1... | collective-permute-start | bytes 49160 | tf_op jit(solution)/shard_map/ppermute | solution.py:14
  6.2 12.5 %collective-permute-start.1 = (f32[2,2,1,1024]{3,2,1,0:T(1,128)S(1)}, f32[2,2,1,1024]{3,2,1,0:T(1,128)S(1)}, u32[]{:S(2)}, u32[]{:S(2)}) collective-permute-start(f32[2,2,1,1024]{3,2,1,0:T(1,128)S(1)} %get-tuple-element.41), channel_id=1, source_target_pairs={{1,0},{2,1},{3,2},{4,3},{5,4},{6,5},{7,6},{8,7},{9,8},{10,9},{11,1... | collective-permute-start | bytes 49160 | tf_op jit(solution)/shard_map/ppermute | solution.py:17
  80.6 6.3 %collective-permute-start.3 = (f32[12,2,1,1024]{3,2,1,0:T(1,128)}, f32[12,2,1,1024]{3,2,1,0:T(1,128)}, u32[]{:S(2)}, u32[]{:S(2)}) collective-permute-start(f32[12,2,1,1024]{3,2,1,0:T(1,128)} %get-tuple-element.38), channel_id=1, source_target_pairs={{0,1},{1,2},{2,3},{3,4},{4,5},{5,6},{6,7},{7,8},{8,9},{9,10},{10,1... | collective-permute-start | bytes 294920 | tf_op jit(solution)/shard_map/ppermute | solution.py:14
  82.5 7.0 %collective-permute-start.2 = (f32[12,2,1,1024]{3,2,1,0:T(1,128)S(1)}, f32[12,2,1,1024]{3,2,1,0:T(1,128)}, u32[]{:S(2)}, u32[]{:S(2)}) collective-permute-start(f32[12,2,1,1024]{3,2,1,0:T(1,128)S(1)} %get-tuple-element.39), channel_id=1, source_target_pairs={{1,0},{2,1},{3,2},{4,3},{5,4},{6,5},{7,6},{8,7},{9,8},{10,9},{11,1... | collective-permute-start | bytes 294920 | tf_op jit(solution)/shard_map/ppermute | solution.py:17
  91.8 6.0 %collective-permute-start.5 = (f32[12,2,1,1024]{3,2,1,0:T(1,128)S(1)}, f32[12,2,1,1024]{3,2,1,0:T(1,128)S(1)}, u32[]{:S(2)}, u32[]{:S(2)}) collective-permute-start(f32[12,2,1,1024]{3,2,1,0:T(1,128)S(1)} %get-tuple-element.36), channel_id=1, source_target_pairs={{0,1},{1,2},{2,3},{3,4},{4,5},{5,6},{6,7},{7,8},{8,9},{9,10},{10,1... | collective-permute-start | bytes 294920 | tf_op jit(solution)/shard_map/ppermute | solution.py:14
  93.7 6.8 %collective-permute-start.4 = (f32[12,2,1,1024]{3,2,1,0:T(1,128)S(1)}, f32[12,2,1,1024]{3,2,1,0:T(1,128)S(1)}, u32[]{:S(2)}, u32[]{:S(2)}) collective-permute-start(f32[12,2,1,1024]{3,2,1,0:T(1,128)S(1)} %get-tuple-element.37), channel_id=1, source_target_pairs={{1,0},{2,1},{3,2},{4,3},{5,4},{6,5},{7,6},{8,7},{9,8},{10,9},{11,1... | collective-permute-start | bytes 294920 | tf_op jit(solution)/shard_map/ppermute | solution.py:17
  101.8 5.2 %collective-permute-start.7 = (f32[12,2,1,1024]{3,2,1,0:T(1,128)S(1)}, f32[12,2,1,1024]{3,2,1,0:T(1,128)S(1)}, u32[]{:S(2)}, u32[]{:S(2)}) collective-permute-start(f32[12,2,1,1024]{3,2,1,0:T(1,128)S(1)} %get-tuple-element.34), channel_id=1, source_target_pairs={{0,1},{1,2},{2,3},{3,4},{4,5},{5,6},{6,7},{7,8},{8,9},{9,10},{10,1... | collective-permute-start | bytes 294920 | tf_op jit(solution)/shard_map/ppermute | solution.py:14
  103.7 6.8 %collective-permute-start.6 = (f32[12,2,1,1024]{3,2,1,0:T(1,128)S(1)}, f32[12,2,1,1024]{3,2,1,0:T(1,128)S(1)}, u32[]{:S(2)}, u32[]{:S(2)}) collective-permute-start(f32[12,2,1,1024]{3,2,1,0:T(1,128)S(1)} %get-tuple-element.35), channel_id=1, source_target_pairs={{1,0},{2,1},{3,2},{4,3},{5,4},{6,5},{7,6},{8,7},{9,8},{10,9},{11,1... | collective-permute-start | bytes 294920 | tf_op jit(solution)/shard_map/ppermute | solution.py:17
  111.9 4.6 %collective-permute-start.9 = (f32[12,2,1,1024]{3,2,1,0:T(1,128)S(1)}, f32[12,2,1,1024]{3,2,1,0:T(1,128)S(1)}, u32[]{:S(2)}, u32[]{:S(2)}) collective-permute-start(f32[12,2,1,1024]{3,2,1,0:T(1,128)S(1)} %get-tuple-element.32), channel_id=1, source_target_pairs={{0,1},{1,2},{2,3},{3,4},{4,5},{5,6},{6,7},{7,8},{8,9},{9,10},{10,1... | collective-permute-start | bytes 294920 | tf_op jit(solution)/shard_map/ppermute | solution.py:14
  113.8 6.8 %collective-permute-start.8 = (f32[12,2,1,1024]{3,2,1,0:T(1,128)S(1)}, f32[12,2,1,1024]{3,2,1,0:T(1,128)S(1)}, u32[]{:S(2)}, u32[]{:S(2)}) collective-permute-start(f32[12,2,1,1024]{3,2,1,0:T(1,128)S(1)} %get-tuple-element.33), channel_id=1, source_target_pairs={{1,0},{2,1},{3,2},{4,3},{5,4},{6,5},{7,6},{8,7},{9,8},{10,9},{11,1... | collective-permute-start | bytes 294920 | tf_op jit(solution)/shard_map/ppermute | solution.py:17
  121.7 62.5 %copy-start.4 = (f32[12,400]{1,0:T(8,128)S(1)}, f32[12,400]{1,0:T(8,128)}, u32[]{:S(2)}) copy-start(f32[12,400]{1,0:T(8,128)} %param.13) | copy-start | bytes 57604
  184.2 7.9 %copy-start.2 = (f32[12,400]{1,0:T(8,128)}, f32[12,400]{1,0:T(8,128)S(1)}, u32[]{:S(2)}) copy-start(f32[12,400]{1,0:T(8,128)S(1)} %psum.7) | copy-start | bytes 57604
  238.9 8.9 %collective-permute-start.11 = (f32[12,2,1,1024]{3,2,1,0:T(1,128)S(1)}, f32[12,2,1,1024]{3,2,1,0:T(1,128)S(1)}, u32[]{:S(2)}, u32[]{:S(2)}) collective-permute-start(f32[12,2,1,1024]{3,2,1,0:T(1,128)S(1)} %get-tuple-element.30), channel_id=1, source_target_pairs={{0,1},{1,2},{2,3},{3,4},{4,5},{5,6},{6,7},{7,8},{8,9},{9,10},{10,1... | collective-permute-start | bytes 294920 | tf_op jit(solution)/shard_map/ppermute | solution.py:14
  243.4 6.8 %collective-permute-start.10 = (f32[12,2,1,1024]{3,2,1,0:T(1,128)S(1)}, f32[12,2,1,1024]{3,2,1,0:T(1,128)S(1)}, u32[]{:S(2)}, u32[]{:S(2)}) collective-permute-start(f32[12,2,1,1024]{3,2,1,0:T(1,128)S(1)} %get-tuple-element.31), channel_id=1, source_target_pairs={{1,0},{2,1},{3,2},{4,3},{5,4},{6,5},{7,6},{8,7},{9,8},{10,9},{11,1... | collective-permute-start | bytes 294920 | tf_op jit(solution)/shard_map/ppermute | solution.py:17
  251.5 5.6 %collective-permute-start.13 = (f32[12,2,1,1024]{3,2,1,0:T(1,128)S(1)}, f32[12,2,1,1024]{3,2,1,0:T(1,128)S(1)}, u32[]{:S(2)}, u32[]{:S(2)}) collective-permute-start(f32[12,2,1,1024]{3,2,1,0:T(1,128)S(1)} %get-tuple-element.28), channel_id=1, source_target_pairs={{0,1},{1,2},{2,3},{3,4},{4,5},{5,6},{6,7},{7,8},{8,9},{9,10},{10,1... | collective-permute-start | bytes 294920 | tf_op jit(solution)/shard_map/ppermute | solution.py:14
  253.4 6.8 %collective-permute-start.12 = (f32[12,2,1,1024]{3,2,1,0:T(1,128)S(1)}, f32[12,2,1,1024]{3,2,1,0:T(1,128)S(1)}, u32[]{:S(2)}, u32[]{:S(2)}) collective-permute-start(f32[12,2,1,1024]{3,2,1,0:T(1,128)S(1)} %get-tuple-element.29), channel_id=1, source_target_pairs={{1,0},{2,1},{3,2},{4,3},{5,4},{6,5},{7,6},{8,7},{9,8},{10,9},{11,1... | collective-permute-start | bytes 294920 | tf_op jit(solution)/shard_map/ppermute | solution.py:17
  261.6 4.4 %collective-permute-start.15 = (f32[12,2,1,1024]{3,2,1,0:T(1,128)S(1)}, f32[12,2,1,1024]{3,2,1,0:T(1,128)S(1)}, u32[]{:S(2)}, u32[]{:S(2)}) collective-permute-start(f32[12,2,1,1024]{3,2,1,0:T(1,128)S(1)} %get-tuple-element.26), channel_id=1, source_target_pairs={{0,1},{1,2},{2,3},{3,4},{4,5},{5,6},{6,7},{7,8},{8,9},{9,10},{10,1... | collective-permute-start | bytes 294920 | tf_op jit(solution)/shard_map/ppermute | solution.py:14
  263.5 6.8 %collective-permute-start.14 = (f32[12,2,1,1024]{3,2,1,0:T(1,128)S(1)}, f32[12,2,1,1024]{3,2,1,0:T(1,128)S(1)}, u32[]{:S(2)}, u32[]{:S(2)}) collective-permute-start(f32[12,2,1,1024]{3,2,1,0:T(1,128)S(1)} %get-tuple-element.27), channel_id=1, source_target_pairs={{1,0},{2,1},{3,2},{4,3},{5,4},{6,5},{7,6},{8,7},{9,8},{10,9},{11,1... | collective-permute-start | bytes 294920 | tf_op jit(solution)/shard_map/ppermute | solution.py:17
  271.6 4.4 %collective-permute-start.17 = (f32[12,2,1,1024]{3,2,1,0:T(1,128)S(1)}, f32[12,2,1,1024]{3,2,1,0:T(1,128)S(1)}, u32[]{:S(2)}, u32[]{:S(2)}) collective-permute-start(f32[12,2,1,1024]{3,2,1,0:T(1,128)S(1)} %get-tuple-element.24), channel_id=1, source_target_pairs={{0,1},{1,2},{2,3},{3,4},{4,5},{5,6},{6,7},{7,8},{8,9},{9,10},{10,1... | collective-permute-start | bytes 294920 | tf_op jit(solution)/shard_map/ppermute | solution.py:14
  273.6 6.8 %collective-permute-start.16 = (f32[12,2,1,1024]{3,2,1,0:T(1,128)S(1)}, f32[12,2,1,1024]{3,2,1,0:T(1,128)S(1)}, u32[]{:S(2)}, u32[]{:S(2)}) collective-permute-start(f32[12,2,1,1024]{3,2,1,0:T(1,128)S(1)} %get-tuple-element.25), channel_id=1, source_target_pairs={{1,0},{2,1},{3,2},{4,3},{5,4},{6,5},{7,6},{8,7},{9,8},{10,9},{11,1... | collective-permute-start | bytes 294920 | tf_op jit(solution)/shard_map/ppermute | solution.py:17
  281.7 5.0 %collective-permute-start.18 = (f32[2,12,2,1,1024]{4,3,2,1,0:T(1,128)S(1)}, f32[2,12,2,1,1024]{4,3,2,1,0:T(1,128)S(1)}, u32[]{:S(2)}, u32[]{:S(2)}) collective-permute-start(f32[2,12,2,1,1024]{4,3,2,1,0:T(1,128)S(1)} %get-tuple-element.22), channel_id=1, source_target_pairs={{0,1},{1,2},{2,3},{3,4},{4,5},{5,6},{6,7},{7,8},{8,9},{9,10},{10,1... | collective-permute-start | bytes 589832 | tf_op jit(solution)/shard_map/ppermute | solution.py:14
  283.7 7.9 %collective-permute-start.19 = (f32[2,12,2,1,1024]{4,3,2,1,0:T(1,128)S(1)}, f32[2,12,2,1,1024]{4,3,2,1,0:T(1,128)S(1)}, u32[]{:S(2)}, u32[]{:S(2)}) collective-permute-start(f32[2,12,2,1,1024]{4,3,2,1,0:T(1,128)S(1)} %get-tuple-element.23), channel_id=1, source_target_pairs={{1,0},{2,1},{3,2},{4,3},{5,4},{6,5},{7,6},{8,7},{9,8},{10,9},{11,1... | collective-permute-start | bytes 589832 | tf_op jit(solution)/shard_map/ppermute | solution.py:17
  (2 other events, 3.8 us)
where the time goes:
time: 296 us; the launch traced here: 294 us
  blocking collectives  108 us (36%)
  other arithmetic  63.4 us (21%)
  starting transfers between devices  53.1 us (18%)
  local copies, waits for them, and re-layouts  32.3 us (11%)
  waiting for transfers between devices  32.2 us (11%)
  between operations  5.11 us (2%)
    psum x1, blocking collectives, local(): predicted = lax.psum(local_heads, 'tile')  49.3 us
    scatter-add x1, other arithmetic, local(): adjoint_source.at[:, :, well_row, well_col]  39.4 us
    pmin x1, blocking collectives, local(): low = lax.pmin(local_low, 'tile')  32.8 us
    ppermute x10, waiting for transfers between devices, extended_2(): lax.ppermute(lax.slice_in_dim(block, 0, width, axis=dim), axis, backward)  32.2 us
    ppermute x10, starting transfers between devices, extended_2(): lax.ppermute(lax.slice_in_dim(block, 0, width, axis=dim), axis, backward)  29.6 us
    pmax x1, blocking collectives, local(): high = lax.pmax(local_high, 'tile')  25.8 us
    ppermute x10, starting transfers between devices, extended_2(): lax.ppermute(lax.slice_in_dim(block, block.shape[dim] - width, None, axis...  23.6 us
    scatter-add x1, local copies, waits for them, and re-layouts, local(): adjoint_source.at[:, :, well_row, well_col]  6.87 us
  transfers between devices with their start and end apart: 20, of which 9 were waited for; matrix products, arithmetic and copies ran while one was open for 4% of the time, Pallas kernels for 0%

commit v1 on v0

--- a/solution.py
+++ b/solution.py
@@ -122,7 +122,7 @@
     heads = solve(recharge[None] + pumping)
     sampled = heads[:, :, well_row, well_col]
     local_heads = jnp.sum(sampled * owned_weight.T[None], axis=1)
-    predicted = lax.psum(local_heads, "tile")
+    predicted = jnp.sum(jax.lax.all_gather(local_heads, axis_name="tile"), axis=0)
     misfit = predicted - observed
     scale = jnp.sqrt(jnp.mean(misfit * misfit) + 1e-06)
     weight = misfit / scale

time: 296 us -> 262 us (0.89)
  blocking collectives: 108 us -> 76.3 us
  starting transfers between devices: 53.1 us -> 47.7 us
  waiting for transfers between devices: 32.2 us -> 35.6 us
    psum x1 -> x0, blocking collectives: 49.3 us -> none  [local(): predicted = lax.psum(local_heads, 'tile')]
    all_gather x0 -> x1, blocking collectives: none -> 17.7 us  [local(): jax.lax.all_gather(local_heads, axis_name='tile')]
    ppermute x10, starting transfers between devices: 29.6 us -> 26.1 us  [extended_2(): lax.ppermute(lax.slice_in_dim(block, 0, width, axis=dim), axis, backward)]
    ppermute x10, waiting for transfers between devices: 32.2 us -> 35.6 us  [extended_2(): lax.ppermute(lax.slice_in_dim(block, 0, width, axis=dim), axis, backward)]
where the time goes in v1:
time: 262 us; the launch traced here: 260 us
  blocking collectives  76.3 us (29%)
  other arithmetic  63.4 us (24%)
  starting transfers between devices  47.7 us (18%)
  waiting for transfers between devices  35.6 us (14%)
  local copies, waits for them, and re-layouts  32.3 us (12%)
  between operations  5.12 us (2%)
    scatter-add x1, other arithmetic, local(): adjoint_source.at[:, :, well_row, well_col]  39.4 us
    ppermute x10, waiting for transfers between devices, extended_2(): lax.ppermute(lax.slice_in_dim(block, 0, width, axis=dim), axis, backward)  35.6 us
    pmin x1, blocking collectives, local(): low = lax.pmin(local_low, 'tile')  32.8 us
    ppermute x10, starting transfers between devices, extended_2(): lax.ppermute(lax.slice_in_dim(block, 0, width, axis=dim), axis, backward)  26.1 us
    pmax x1, blocking collectives, local(): high = lax.pmax(local_high, 'tile')  25.8 us
    ppermute x10, starting transfers between devices, extended_2(): lax.ppermute(lax.slice_in_dim(block, block.shape[dim] - width, None, axis...  21.5 us
    all_gather x1, blocking collectives, local(): jax.lax.all_gather(local_heads, axis_name='tile')  17.7 us
    scatter-add x1, local copies, waits for them, and re-layouts, local(): adjoint_source.at[:, :, well_row, well_col]  6.87 us
  transfers between devices with their start and end apart: 20, of which 9 were waited for; matrix products, arithmetic and copies ran while one was open for 4% of the time, Pallas kernels for 0%

profile of v1, /device:TPU:5, one launch (start us, length us, event | category | flops | bytes accessed | tf_op | source)
XLA Modules:
  0.0 260.5 jit_solution(7928543162460211259)
XLA Ops:
  2.5 3.7 %collective-permute-start = (f32[2,2,1,1024]{3,2,1,0:T(1,128)S(1)}, f32[2,2,1,1024]{3,2,1,0:T(1,128)S(1)}, u32[]{:S(2)}, u32[]{:S(2)}) collective-permute-start(f32[2,2,1,1024]{3,2,1,0:T(1,128)S(1)} %get-tuple-element.38), channel_id=1, source_target_pairs={{0,1},{1,2},{2,3},{3,4},{4,5},{5,6},{6,7},{7,8},{8,9},{9,10},{10,1... | collective-permute-start | bytes 49160 | tf_op jit(solution)/shard_map/ppermute | solution.py:14
  15.8 2.9 %scatter_fusion = f32[12,2,8,1024]{3,2,1,0:T(8,128)S(1)} fusion(f32[12,2,8,1024]{3,2,1,0:T(8,128)S(1)} %add.279, s32[24]{0:T(128)S(1)} %reshape.153, f32[24]{0:T(128)S(1)} %reshape.155), kind=kCustom, calls=%fused_computation.4 | custom fusion | flops 24 | bytes 672 | tf_op jit(solution)/shard_map/scatter-add | solution.py:121
  19.5 25.8 %pmax.7 = f32[]{:T(128)} all-reduce(f32[]{:T(128)} %get-tuple-element.3), channel_id=1, replica_groups=mesh['groups'=2,'tile'=16] {'tile'}, use_global_device_ids=true, to_apply=%region_2.3 | all-reduce | flops 1 | bytes 8 | tf_op jit(solution)/shard_map/pmax | solution.py:93
  45.4 32.8 %pmin.7 = f32[]{:T(128)} all-reduce(f32[]{:T(128)} %get-tuple-element.2), channel_id=1, replica_groups=mesh['groups'=2,'tile'=16] {'tile'}, use_global_device_ids=true, to_apply=%region_4.5 | all-reduce | flops 1 | bytes 8 | tf_op jit(solution)/shard_map/pmin | solution.py:94
  82.5 2.6 collective-permute-start.2
  86.9 2.7 %collective-permute-done.2 = f32[12,2,1,1024]{3,2,1,0:T(1,128)} collective-permute-done((f32[12,2,1,1024]{3,2,1,0:T(1,128)S(1)}, f32[12,2,1,1024]{3,2,1,0:T(1,128)}, u32[]{:S(2)}, u32[]{:S(2)}) %collective-permute-start.2) | collective-permute-done | bytes 98336 | tf_op jit(solution)/shard_map/ppermute | solution.py:17
  93.7 4.0 %collective-permute-start.4 = (f32[12,2,1,1024]{3,2,1,0:T(1,128)S(1)}, f32[12,2,1,1024]{3,2,1,0:T(1,128)S(1)}, u32[]{:S(2)}, u32[]{:S(2)}) collective-permute-start(f32[12,2,1,1024]{3,2,1,0:T(1,128)S(1)} %get-tuple-element.35), channel_id=1, source_target_pairs={{1,0},{2,1},{3,2},{4,3},{5,4},{6,5},{7,6},{8,7},{9,8},{10,9},{11,1... | collective-permute-start | bytes 294920 | tf_op jit(solution)/shard_map/ppermute | solution.py:17
  97.8 2.7 %collective-permute-done.4 = f32[12,2,1,1024]{3,2,1,0:T(1,128)S(1)} collective-permute-done((f32[12,2,1,1024]{3,2,1,0:T(1,128)S(1)}, f32[12,2,1,1024]{3,2,1,0:T(1,128)S(1)}, u32[]{:S(2)}, u32[]{:S(2)}) %collective-permute-start.4) | collective-permute-done | bytes 98336 | tf_op jit(solution)/shard_map/ppermute | solution.py:17
  103.7 3.3 %collective-permute-start.6 = (f32[12,2,1,1024]{3,2,1,0:T(1,128)S(1)}, f32[12,2,1,1024]{3,2,1,0:T(1,128)S(1)}, u32[]{:S(2)}, u32[]{:S(2)}) collective-permute-start(f32[12,2,1,1024]{3,2,1,0:T(1,128)S(1)} %get-tuple-element.33), channel_id=1, source_target_pairs={{1,0},{2,1},{3,2},{4,3},{5,4},{6,5},{7,6},{8,7},{9,8},{10,9},{11,1... | collective-permute-start | bytes 294920 | tf_op jit(solution)/shard_map/ppermute | solution.py:17
  107.1 3.5 %collective-permute-done.6 = f32[12,2,1,1024]{3,2,1,0:T(1,128)S(1)} collective-permute-done((f32[12,2,1,1024]{3,2,1,0:T(1,128)S(1)}, f32[12,2,1,1024]{3,2,1,0:T(1,128)S(1)}, u32[]{:S(2)}, u32[]{:S(2)}) %collective-permute-start.6) | collective-permute-done | bytes 98336 | tf_op jit(solution)/shard_map/ppermute | solution.py:17
  113.8 2.6 collective-permute-start.8
  116.4 4.2 %collective-permute-done.8 = f32[12,2,1,1024]{3,2,1,0:T(1,128)S(1)} collective-permute-done((f32[12,2,1,1024]{3,2,1,0:T(1,128)S(1)}, f32[12,2,1,1024]{3,2,1,0:T(1,128)S(1)}, u32[]{:S(2)}, u32[]{:S(2)}) %collective-permute-start.8) | collective-permute-done | bytes 98336 | tf_op jit(solution)/shard_map/ppermute | solution.py:17
  121.7 5.9 %copy.25 = f32[12,2,8,1024]{0,1,3,2:T(2,128)} copy(f32[12,2,8,1024]{3,2,1,0:T(8,128)S(1)} %fusion.31) | data formatting | bytes 1572864 | tf_op jit(solution)/shard_map/add | solution.py:63
  127.6 6.5 %gather_fusion.3 = f32[400,12,2]{1,2,0:T(2,128)S(1)} fusion(f32[12,2,8,1024]{0,1,3,2:T(2,128)} %copy.25, s32[400]{0:T(512)S(1)} %bitcast.32), kind=kCustom, calls=%fused_computation.3 | custom fusion | bytes 80000 | tf_op jit(solution)/shard_map/gather | solution.py:123
  134.9 17.7 %all-gather.1 = f32[16,12,400]{2,1,0:T(8,128)S(1)} all-gather(f32[1,12,400]{2,1,0:T(8,128)S(1)} %copy.27), channel_id=2, replica_groups=mesh['groups'=2,'tile'=16] {'tile'}, dimensions={0}, use_global_device_ids=true | all-gather | bytes 326400 | tf_op jit(solution)/shard_map/all_gather | solution.py:125
  154.6 5.9 %broadcast.196 = f32[12,2,8,1024]{0,1,3,2:T(2,128)} broadcast(f32[]{:T(128)} %constant.19.clone.1), dimensions={} | broadcast | bytes 786436 | tf_op jit(solution)/shard_map/broadcast.24
  160.5 39.4 %scatter_fusion.1 = f32[12,2,8,1024]{0,1,3,2:T(2,128)} fusion(f32[12,2,8,1024]{0,1,3,2:T(2,128)} %broadcast.196, s32[400]{0:T(512)S(1)} %bitcast.33, f32[400,12,2]{1,2,0:T(2,128)S(1)} %multiply_bitcast_fusion), kind=kCustom, calls=%fused_computation.5 | custom fusion | flops 9600 | bytes 118400 | tf_op jit(solution)/shard_map/scatter-add | solution.py:130
  199.9 6.9 %copy.29 = f32[12,2,8,1024]{3,2,1,0:T(8,128)S(1)} copy(f32[12,2,8,1024]{0,1,3,2:T(2,128)} %scatter_fusion.1) | data formatting | bytes 1572864 | tf_op jit(solution)/shard_map/scatter-add | solution.py:130
  211.8 4.8 %collective-permute-done.10 = f32[12,2,1,1024]{3,2,1,0:T(1,128)S(1)} collective-permute-done((f32[12,2,1,1024]{3,2,1,0:T(1,128)S(1)}, f32[12,2,1,1024]{3,2,1,0:T(1,128)S(1)}, u32[]{:S(2)}, u32[]{:S(2)}) %collective-permute-start.10) | collective-permute-done | bytes 98336 | tf_op jit(solution)/shard_map/ppermute | solution.py:17
  219.8 2.6 %collective-permute-start.12 = (f32[12,2,1,1024]{3,2,1,0:T(1,128)S(1)}, f32[12,2,1,1024]{3,2,1,0:T(1,128)S(1)}, u32[]{:S(2)}, u32[]{:S(2)}) collective-permute-start(f32[12,2,1,1024]{3,2,1,0:T(1,128)S(1)} %get-tuple-element.27), channel_id=1, source_target_pairs={{1,0},{2,1},{3,2},{4,3},{5,4},{6,5},{7,6},{8,7},{9,8},{10,9},{11,1... | collective-permute-start | bytes 294920 | tf_op jit(solution)/shard_map/ppermute | solution.py:17
  222.5 4.1 %collective-permute-done.12 = f32[12,2,1,1024]{3,2,1,0:T(1,128)S(1)} collective-permute-done((f32[12,2,1,1024]{3,2,1,0:T(1,128)S(1)}, f32[12,2,1,1024]{3,2,1,0:T(1,128)S(1)}, u32[]{:S(2)}, u32[]{:S(2)}) %collective-permute-start.12) | collective-permute-done | bytes 98336 | tf_op jit(solution)/shard_map/ppermute | solution.py:17
  232.4 4.4 %collective-permute-done.14 = f32[12,2,1,1024]{3,2,1,0:T(1,128)S(1)} collective-permute-done((f32[12,2,1,1024]{3,2,1,0:T(1,128)S(1)}, f32[12,2,1,1024]{3,2,1,0:T(1,128)S(1)}, u32[]{:S(2)}, u32[]{:S(2)}) %collective-permute-start.14) | collective-permute-done | bytes 98336 | tf_op jit(solution)/shard_map/ppermute | solution.py:17
  242.5 4.4 %collective-permute-done.16 = f32[12,2,1,1024]{3,2,1,0:T(1,128)S(1)} collective-permute-done((f32[12,2,1,1024]{3,2,1,0:T(1,128)S(1)}, f32[12,2,1,1024]{3,2,1,0:T(1,128)S(1)}, u32[]{:S(2)}, u32[]{:S(2)}) %collective-permute-start.16) | collective-permute-done | bytes 98336 | tf_op jit(solution)/shard_map/ppermute | solution.py:17
  253.2 4.8 %collective-permute-done.19 = f32[2,12,2,1,1024]{4,3,2,1,0:T(1,128)S(1)} collective-permute-done((f32[2,12,2,1,1024]{4,3,2,1,0:T(1,128)S(1)}, f32[2,12,2,1,1024]{4,3,2,1,0:T(1,128)S(1)}, u32[]{:S(2)}, u32[]{:S(2)}) %collective-permute-start.19) | collective-permute-done | bytes 196640 | tf_op jit(solution)/shard_map/ppermute | solution.py:17
  (123 shorter events, 57.2 us)
Async XLA Ops:
  0.6 13.9 %copy-start.5 = (f32[12]{0:T(128)S(1)}, f32[12]{0:T(128)}, u32[]{:S(2)}) copy-start(f32[12]{0:T(128)} %param.14) | copy-start | bytes 148
  0.6 15.1 %copy-start.3 = (f32[2,8,1024]{2,1,0:T(8,128)S(1)}, f32[2,8,1024]{2,1,0:T(8,128)}, u32[]{:S(2)}) copy-start(f32[2,8,1024]{2,1,0:T(8,128)} %param.12) | copy-start | bytes 196612
  2.5 16.2 %collective-permute-start = (f32[2,2,1,1024]{3,2,1,0:T(1,128)S(1)}, f32[2,2,1,1024]{3,2,1,0:T(1,128)S(1)}, u32[]{:S(2)}, u32[]{:S(2)}) collective-permute-start(f32[2,2,1,1024]{3,2,1,0:T(1,128)S(1)} %get-tuple-element.38), channel_id=1, source_target_pairs={{0,1},{1,2},{2,3},{3,4},{4,5},{5,6},{6,7},{7,8},{8,9},{9,10},{10,1... | collective-permute-start | bytes 49160 | tf_op jit(solution)/shard_map/ppermute | solution.py:14
  6.2 12.5 %collective-permute-start.1 = (f32[2,2,1,1024]{3,2,1,0:T(1,128)S(1)}, f32[2,2,1,1024]{3,2,1,0:T(1,128)S(1)}, u32[]{:S(2)}, u32[]{:S(2)}) collective-permute-start(f32[2,2,1,1024]{3,2,1,0:T(1,128)S(1)} %get-tuple-element.39), channel_id=1, source_target_pairs={{1,0},{2,1},{3,2},{4,3},{5,4},{6,5},{7,6},{8,7},{9,8},{10,9},{11,1... | collective-permute-start | bytes 49160 | tf_op jit(solution)/shard_map/ppermute | solution.py:17
  80.6 6.3 %collective-permute-start.3 = (f32[12,2,1,1024]{3,2,1,0:T(1,128)}, f32[12,2,1,1024]{3,2,1,0:T(1,128)}, u32[]{:S(2)}, u32[]{:S(2)}) collective-permute-start(f32[12,2,1,1024]{3,2,1,0:T(1,128)} %get-tuple-element.36), channel_id=1, source_target_pairs={{0,1},{1,2},{2,3},{3,4},{4,5},{5,6},{6,7},{7,8},{8,9},{9,10},{10,1... | collective-permute-start | bytes 294920 | tf_op jit(solution)/shard_map/ppermute | solution.py:14
  82.5 7.0 %collective-permute-start.2 = (f32[12,2,1,1024]{3,2,1,0:T(1,128)S(1)}, f32[12,2,1,1024]{3,2,1,0:T(1,128)}, u32[]{:S(2)}, u32[]{:S(2)}) collective-permute-start(f32[12,2,1,1024]{3,2,1,0:T(1,128)S(1)} %get-tuple-element.37), channel_id=1, source_target_pairs={{1,0},{2,1},{3,2},{4,3},{5,4},{6,5},{7,6},{8,7},{9,8},{10,9},{11,1... | collective-permute-start | bytes 294920 | tf_op jit(solution)/shard_map/ppermute | solution.py:17
  91.8 6.0 %collective-permute-start.5 = (f32[12,2,1,1024]{3,2,1,0:T(1,128)S(1)}, f32[12,2,1,1024]{3,2,1,0:T(1,128)S(1)}, u32[]{:S(2)}, u32[]{:S(2)}) collective-permute-start(f32[12,2,1,1024]{3,2,1,0:T(1,128)S(1)} %get-tuple-element.34), channel_id=1, source_target_pairs={{0,1},{1,2},{2,3},{3,4},{4,5},{5,6},{6,7},{7,8},{8,9},{9,10},{10,1... | collective-permute-start | bytes 294920 | tf_op jit(solution)/shard_map/ppermute | solution.py:14
  93.7 6.8 %collective-permute-start.4 = (f32[12,2,1,1024]{3,2,1,0:T(1,128)S(1)}, f32[12,2,1,1024]{3,2,1,0:T(1,128)S(1)}, u32[]{:S(2)}, u32[]{:S(2)}) collective-permute-start(f32[12,2,1,1024]{3,2,1,0:T(1,128)S(1)} %get-tuple-element.35), channel_id=1, source_target_pairs={{1,0},{2,1},{3,2},{4,3},{5,4},{6,5},{7,6},{8,7},{9,8},{10,9},{11,1... | collective-permute-start | bytes 294920 | tf_op jit(solution)/shard_map/ppermute | solution.py:17
  101.8 5.2 %collective-permute-start.7 = (f32[12,2,1,1024]{3,2,1,0:T(1,128)S(1)}, f32[12,2,1,1024]{3,2,1,0:T(1,128)S(1)}, u32[]{:S(2)}, u32[]{:S(2)}) collective-permute-start(f32[12,2,1,1024]{3,2,1,0:T(1,128)S(1)} %get-tuple-element.32), channel_id=1, source_target_pairs={{0,1},{1,2},{2,3},{3,4},{4,5},{5,6},{6,7},{7,8},{8,9},{9,10},{10,1... | collective-permute-start | bytes 294920 | tf_op jit(solution)/shard_map/ppermute | solution.py:14
  103.7 6.8 %collective-permute-start.6 = (f32[12,2,1,1024]{3,2,1,0:T(1,128)S(1)}, f32[12,2,1,1024]{3,2,1,0:T(1,128)S(1)}, u32[]{:S(2)}, u32[]{:S(2)}) collective-permute-start(f32[12,2,1,1024]{3,2,1,0:T(1,128)S(1)} %get-tuple-element.33), channel_id=1, source_target_pairs={{1,0},{2,1},{3,2},{4,3},{5,4},{6,5},{7,6},{8,7},{9,8},{10,9},{11,1... | collective-permute-start | bytes 294920 | tf_op jit(solution)/shard_map/ppermute | solution.py:17
  111.9 4.6 %collective-permute-start.9 = (f32[12,2,1,1024]{3,2,1,0:T(1,128)S(1)}, f32[12,2,1,1024]{3,2,1,0:T(1,128)S(1)}, u32[]{:S(2)}, u32[]{:S(2)}) collective-permute-start(f32[12,2,1,1024]{3,2,1,0:T(1,128)S(1)} %get-tuple-element.30), channel_id=1, source_target_pairs={{0,1},{1,2},{2,3},{3,4},{4,5},{5,6},{6,7},{7,8},{8,9},{9,10},{10,1... | collective-permute-start | bytes 294920 | tf_op jit(solution)/shard_map/ppermute | solution.py:14
  113.8 6.8 %collective-permute-start.8 = (f32[12,2,1,1024]{3,2,1,0:T(1,128)S(1)}, f32[12,2,1,1024]{3,2,1,0:T(1,128)S(1)}, u32[]{:S(2)}, u32[]{:S(2)}) collective-permute-start(f32[12,2,1,1024]{3,2,1,0:T(1,128)S(1)} %get-tuple-element.31), channel_id=1, source_target_pairs={{1,0},{2,1},{3,2},{4,3},{5,4},{6,5},{7,6},{8,7},{9,8},{10,9},{11,1... | collective-permute-start | bytes 294920 | tf_op jit(solution)/shard_map/ppermute | solution.py:17
  127.6 25.0 %copy-start.4 = (f32[12,400]{1,0:T(8,128)S(1)}, f32[12,400]{1,0:T(8,128)}, u32[]{:S(2)}) copy-start(f32[12,400]{1,0:T(8,128)} %param.13) | copy-start | bytes 57604
  152.6 7.9 %copy-start.2 = (f32[12,400]{1,0:T(8,128)}, f32[12,400]{1,0:T(8,128)S(1)}, u32[]{:S(2)}) copy-start(f32[12,400]{1,0:T(8,128)S(1)} %reduce_sum.57) | copy-start | bytes 57604
  207.3 4.5 %collective-permute-start.11 = (f32[12,2,1,1024]{3,2,1,0:T(1,128)S(1)}, f32[12,2,1,1024]{3,2,1,0:T(1,128)S(1)}, u32[]{:S(2)}, u32[]{:S(2)}) collective-permute-start(f32[12,2,1,1024]{3,2,1,0:T(1,128)S(1)} %get-tuple-element.28), channel_id=1, source_target_pairs={{0,1},{1,2},{2,3},{3,4},{4,5},{5,6},{6,7},{7,8},{8,9},{9,10},{10,1... | collective-permute-start | bytes 294920 | tf_op jit(solution)/shard_map/ppermute | solution.py:14
  209.8 6.8 %collective-permute-start.10 = (f32[12,2,1,1024]{3,2,1,0:T(1,128)S(1)}, f32[12,2,1,1024]{3,2,1,0:T(1,128)S(1)}, u32[]{:S(2)}, u32[]{:S(2)}) collective-permute-start(f32[12,2,1,1024]{3,2,1,0:T(1,128)S(1)} %get-tuple-element.29), channel_id=1, source_target_pairs={{1,0},{2,1},{3,2},{4,3},{5,4},{6,5},{7,6},{8,7},{9,8},{10,9},{11,1... | collective-permute-start | bytes 294920 | tf_op jit(solution)/shard_map/ppermute | solution.py:17
  217.9 4.6 %collective-permute-start.13 = (f32[12,2,1,1024]{3,2,1,0:T(1,128)S(1)}, f32[12,2,1,1024]{3,2,1,0:T(1,128)S(1)}, u32[]{:S(2)}, u32[]{:S(2)}) collective-permute-start(f32[12,2,1,1024]{3,2,1,0:T(1,128)S(1)} %get-tuple-element.26), channel_id=1, source_target_pairs={{0,1},{1,2},{2,3},{3,4},{4,5},{5,6},{6,7},{7,8},{8,9},{9,10},{10,1... | collective-permute-start | bytes 294920 | tf_op jit(solution)/shard_map/ppermute | solution.py:14
  219.8 6.8 %collective-permute-start.12 = (f32[12,2,1,1024]{3,2,1,0:T(1,128)S(1)}, f32[12,2,1,1024]{3,2,1,0:T(1,128)S(1)}, u32[]{:S(2)}, u32[]{:S(2)}) collective-permute-start(f32[12,2,1,1024]{3,2,1,0:T(1,128)S(1)} %get-tuple-element.27), channel_id=1, source_target_pairs={{1,0},{2,1},{3,2},{4,3},{5,4},{6,5},{7,6},{8,7},{9,8},{10,9},{11,1... | collective-permute-start | bytes 294920 | tf_op jit(solution)/shard_map/ppermute | solution.py:17
  228.0 4.4 %collective-permute-start.15 = (f32[12,2,1,1024]{3,2,1,0:T(1,128)S(1)}, f32[12,2,1,1024]{3,2,1,0:T(1,128)S(1)}, u32[]{:S(2)}, u32[]{:S(2)}) collective-permute-start(f32[12,2,1,1024]{3,2,1,0:T(1,128)S(1)} %get-tuple-element.24), channel_id=1, source_target_pairs={{0,1},{1,2},{2,3},{3,4},{4,5},{5,6},{6,7},{7,8},{8,9},{9,10},{10,1... | collective-permute-start | bytes 294920 | tf_op jit(solution)/shard_map/ppermute | solution.py:14
  229.9 6.8 %collective-permute-start.14 = (f32[12,2,1,1024]{3,2,1,0:T(1,128)S(1)}, f32[12,2,1,1024]{3,2,1,0:T(1,128)S(1)}, u32[]{:S(2)}, u32[]{:S(2)}) collective-permute-start(f32[12,2,1,1024]{3,2,1,0:T(1,128)S(1)} %get-tuple-element.25), channel_id=1, source_target_pairs={{1,0},{2,1},{3,2},{4,3},{5,4},{6,5},{7,6},{8,7},{9,8},{10,9},{11,1... | collective-permute-start | bytes 294920 | tf_op jit(solution)/shard_map/ppermute | solution.py:17
  238.1 4.4 %collective-permute-start.17 = (f32[12,2,1,1024]{3,2,1,0:T(1,128)S(1)}, f32[12,2,1,1024]{3,2,1,0:T(1,128)S(1)}, u32[]{:S(2)}, u32[]{:S(2)}) collective-permute-start(f32[12,2,1,1024]{3,2,1,0:T(1,128)S(1)} %get-tuple-element.22), channel_id=1, source_target_pairs={{0,1},{1,2},{2,3},{3,4},{4,5},{5,6},{6,7},{7,8},{8,9},{9,10},{10,1... | collective-permute-start | bytes 294920 | tf_op jit(solution)/shard_map/ppermute | solution.py:14
  240.0 6.8 %collective-permute-start.16 = (f32[12,2,1,1024]{3,2,1,0:T(1,128)S(1)}, f32[12,2,1,1024]{3,2,1,0:T(1,128)S(1)}, u32[]{:S(2)}, u32[]{:S(2)}) collective-permute-start(f32[12,2,1,1024]{3,2,1,0:T(1,128)S(1)} %get-tuple-element.23), channel_id=1, source_target_pairs={{1,0},{2,1},{3,2},{4,3},{5,4},{6,5},{7,6},{8,7},{9,8},{10,9},{11,1... | collective-permute-start | bytes 294920 | tf_op jit(solution)/shard_map/ppermute | solution.py:17
  248.1 5.0 %collective-permute-start.18 = (f32[2,12,2,1,1024]{4,3,2,1,0:T(1,128)S(1)}, f32[2,12,2,1,1024]{4,3,2,1,0:T(1,128)S(1)}, u32[]{:S(2)}, u32[]{:S(2)}) collective-permute-start(f32[2,12,2,1,1024]{4,3,2,1,0:T(1,128)S(1)} %get-tuple-element.20), channel_id=1, source_target_pairs={{0,1},{1,2},{2,3},{3,4},{4,5},{5,6},{6,7},{7,8},{8,9},{9,10},{10,1... | collective-permute-start | bytes 589832 | tf_op jit(solution)/shard_map/ppermute | solution.py:14
  250.1 7.9 %collective-permute-start.19 = (f32[2,12,2,1,1024]{4,3,2,1,0:T(1,128)S(1)}, f32[2,12,2,1,1024]{4,3,2,1,0:T(1,128)S(1)}, u32[]{:S(2)}, u32[]{:S(2)}) collective-permute-start(f32[2,12,2,1,1024]{4,3,2,1,0:T(1,128)S(1)} %get-tuple-element.21), channel_id=1, source_target_pairs={{1,0},{2,1},{3,2},{4,3},{5,4},{6,5},{7,6},{8,7},{9,8},{10,9},{11,1... | collective-permute-start | bytes 589832 | tf_op jit(solution)/shard_map/ppermute | solution.py:17
  (2 other events, 3.8 us)
